TPU v7x, 128 devices: a whole 4x4x4 slice. The times are simulated.
128 devices in a mesh: patch: 16 (over z, x_hi, core), head: 8 (over x_lo, y).
Axes of the slice: x: 4 (x_hi: 2, x_lo: 2; x = x_hi * 2 + x_lo), y: 4, z: 4, core: 2. Of those that a mesh axis runs over, the one named last changes fastest.
Arguments:
- hidden_in: bfloat16 [8192, 5120], P('patch', 'head'), may hold values from -6 to 6
- positions: int32 [8192], P('patch'), may hold values from 0 to 8191, each once
- modulation: float32 [3, 5120], replicated, may hold values from -4 to 4
- w_qkv: bfloat16 [5120, 3, 3072], P(None, None, 'head'), may hold values from -1 to 1
- qk_gain: float32 [2, 3072], P(None, 'head'), may hold values from 1.5 to 4
- w_out: bfloat16 [3072, 5120], P('head'), may hold values from -0.109375 to 0.109375
- stale_kv: bfloat16 [8192, 2, 3072], P('patch', None, 'head'), may hold values from -500 to 500
Outputs:
- hidden_out: bfloat16 [8192, 5120], P('patch', 'head')
Inputs may be any that keep to these rules, and one draw needn't show every extreme that they name: `positions`: every position of 0 to 8191 is held by exactly one row.
All inputs are finite; a program needn't handle non-finite values.
Results may differ from a plain program's by a relative error of at most 0.02.
The roundings to bfloat16 on the way count: a program that leaves them out, or rounds other values in their place, can miss the bound.
Values may be sent and summed in bfloat16 or wider, within the bound.
A program may use at most 192 MiB of HBM per device.

v0:
```python
import jax
import jax.numpy as jnp
from jax import lax
from jax.sharding import PartitionSpec as P

HD = 128


def rotate_pairs(values_in, positions):
    half_dim = values_in.shape[-1] // 2
    inverse_freq = 10000.0 ** (-2.0 * jnp.arange(half_dim, dtype=jnp.float32) / values_in.shape[-1])
    angles = positions.astype(jnp.float32)[:, None] * inverse_freq[None, :]
    cosine = jnp.cos(angles)[:, None, :]
    sine_part = jnp.sin(angles)[:, None, :]
    first_half = values_in[..., :half_dim]
    second_half = values_in[..., half_dim:]
    return jnp.concatenate(
        [
            first_half * cosine - second_half * sine_part,
            first_half * sine_part + second_half * cosine,
        ],
        axis=-1,
    )


def local(hidden_in, positions, modulation, w_qkv, qk_gain, w_out, stale_kv):
    row_count, local_width = hidden_in.shape
    gathered_in = lax.all_gather(hidden_in, "head", axis=1, tiled=True)
    features = gathered_in.astype(jnp.float32)
    centered = features - jnp.mean(features, axis=-1, keepdims=True)
    variance = jnp.mean(centered * centered, axis=-1, keepdims=True)
    modulated = (
        centered * lax.rsqrt(variance + 1e-06) * (1.0 + modulation[1]) + modulation[0]
    ).astype(jnp.bfloat16)
    projected = jnp.einsum("td,dcf->tcf", modulated, w_qkv, preferred_element_type=jnp.float32)
    head_width = w_qkv.shape[2]
    head_count = head_width // HD
    queries = projected[:, 0]
    keys_new = projected[:, 1]
    fresh_values = projected[:, 2].astype(jnp.bfloat16)
    squares = lax.psum(
        (jnp.sum(queries * queries, axis=-1), jnp.sum(keys_new * keys_new, axis=-1)), "head"
    )
    total_width = head_width * lax.axis_size("head")
    queries = queries * lax.rsqrt(squares[0][:, None] / total_width + 1e-06) * qk_gain[0]
    keys_new = keys_new * lax.rsqrt(squares[1][:, None] / total_width + 1e-06) * qk_gain[1]
    rotated_queries = rotate_pairs(queries.reshape(row_count, head_count, HD), positions).astype(
        jnp.bfloat16
    )
    rotated_keys = rotate_pairs(keys_new.reshape(row_count, head_count, HD), positions).astype(
        jnp.bfloat16
    )
    scaling = HD ** (-0.5)
    own_start = lax.axis_index("patch") * row_count
    stale_all = lax.all_gather(stale_kv, "patch", axis=0, tiled=True)
    fresh_table = jnp.stack([rotated_keys.reshape(row_count, head_width), fresh_values], axis=1)
    merged_rows = lax.dynamic_update_slice(
        stale_all, fresh_table, (own_start, jnp.int32(0), jnp.int32(0))
    )
    key_rows = merged_rows[:, 0].reshape(-1, head_count, HD)
    value_rows = merged_rows[:, 1].reshape(-1, head_count, HD)
    scores = (
        jnp.einsum("qhd,khd->qhk", rotated_queries, key_rows, preferred_element_type=jnp.float32)
        * scaling
    )
    row_max = jnp.max(scores, axis=-1, keepdims=True)
    weights = jnp.exp(scores - row_max)
    totals = jnp.sum(weights, axis=-1)
    summed_values = jnp.einsum(
        "qhk,khd->qhd", weights.astype(jnp.bfloat16), value_rows, preferred_element_type=jnp.float32
    )
    attended_f = summed_values / totals[..., None]
    attended = attended_f.astype(jnp.bfloat16).reshape(row_count, head_width)
    partial_out = jnp.dot(attended, w_out, preferred_element_type=jnp.float32)
    attention_out = lax.psum_scatter(
        partial_out.astype(jnp.bfloat16), "head", scatter_dimension=1, tiled=True
    ).astype(jnp.float32)
    gate_slice = lax.dynamic_slice_in_dim(
        modulation[2], lax.axis_index("head") * local_width, local_width
    )
    return (hidden_in.astype(jnp.float32) + gate_slice * attention_out).astype(jnp.bfloat16)


def solution(mesh):
    return jax.shard_map(
        local,
        mesh=mesh,
        in_specs=(
            P("patch", "head"),
            P("patch"),
            P(),
            P(None, None, "head"),
            P(None, "head"),
            P("head", None),
            P("patch", None, "head"),
        ),
        out_specs=P("patch", "head"),
        check_vma=False,
    )
```

profile of v0, /device:TPU:1, one launch (start us, length us, event | category | flops | bytes accessed | tf_op | source)
XLA Modules:
  0.0 325.7 jit_solution(15649707241687997433)
XLA Ops:
  6.5 0.7 all-gather.5.cloned.1.call-update
  7.3 3.1 copy.22
  11.1 0.8 slice_reduce_fusion
  11.9 1.8 multiply_cosine_fusion
  13.7 1.1 fusion.30
  14.8 59.9 %all-gather.5.cloned.1.call-done = bf16[512,5120]{1,0:T(8,128)(2,1)} async-done(((bf16[512,640]{1,0:T(8,128)(2,1)}), bf16[512,5120]{1,0:T(8,128)(2,1)}) %all-gather.5.cloned.1.call-update) | async-done | bytes 5242896 | tf_op jit(solution)/shard_map/all_gather | solution.py:28
  74.7 3.4 %convert_reduce_fusion = f32[512]{0:T(512)S(1)} fusion(bf16[512,5120]{1,0:T(8,128)(2,1)} %all-gather.5.cloned.1.call-done), kind=kLoop, calls=%fused_computation.7 | loop fusion | flops 5242368 | bytes 5244928 | tf_op jit(solution)/shard_map/reduce_sum | solution.py:30
  78.1 4.0 %fusion.7 = f32[512]{0:T(512)S(1)} fusion(bf16[512,5120]{1,0:T(8,128)(2,1)} %all-gather.5.cloned.1.call-done, f32[512]{0:T(512)S(1)} %broadcast_multiply_fusion), kind=kLoop, calls=%fused_computation.10 | loop fusion | flops 10485248 | bytes 5246976 | tf_op jit(solution)/shard_map/reduce_sum | solution.py:31
  82.1 11.5 %fusion.12 = f32[512,3,384]{0,2,1:T(8,128)S(1)} fusion(bf16[5120,3,384]{2,0,1:T(8,128)(2,1)} %param.10, bf16[512,5120]{1,0:T(8,128)(2,1)S(1)} %copy-done, f32[5120]{0:T(1024)S(1)} %bitcast.46, f32[5120]{0:T(1024)S(1)} %bitcast.47, f32[512]{0:T(512)S(1)} %add_rsqrt_fusion.2, f32[512]{0:T(512)S(1)} %broadcast_multiply_fusion), kind=kOutput, calls=%fused_computation.16 | convolution fusion | flops 6055526400 | bytes 19443712 | tf_op jit(solution)/shard_map/td,dcf->tcf/dot_general | solution.py:35
  93.6 1.4 copy-done.3
  95.1 1.6 multiply_reduce_fusion
  97.3 12.8 %all-reduce = (f32[512]{0:T(512)S(1)}, f32[512]{0:T(512)S(1)}) all-reduce(f32[512]{0:T(512)S(1)} %get-tuple-element.6, f32[512]{0:T(512)S(1)} %get-tuple-element.5), channel_id=1, replica_groups=mesh['patch'=16,'head'=8] {'head'}, use_global_device_ids=true, to_apply=%region_3.0 | all-reduce | flops 1024 | bytes 8192 | tf_op jit(solution)/shard_map/psum | solution.py:41
  110.4 1.6 subtract_convert_fusion
  112.4 62.0 %all-gather.3.cloned.1.call-done = bf16[8192,2,384]{0,2,1:T(8,128)(2,1)} async-done(((bf16[512,2,384]{0,2,1:T(8,128)(2,1)}), bf16[8192,2,384]{0,2,1:T(8,128)(2,1)}) %all-gather.3.cloned.1.call-update) | async-done | bytes 12582928 | tf_op jit(solution)/shard_map/all_gather | solution.py:55
  174.4 1.0 maximum_dynamic-update-slice_fusion
  175.4 8.2 %fusion.29 = (bf16[8192,1,384]{0,2,1:T(8,128)(2,1)S(1)}, bf16[8192,1,384]{0,2,1:T(8,128)(2,1)}) fusion(bf16[8192,2,384]{0,2,1:T(8,128)(2,1)} %maximum_dynamic-update-slice_fusion), kind=kLoop, calls=%fused_computation.52 | loop fusion | bytes 25165824 | tf_op jit(solution)/shard_map/slice | solution.py:60
  183.6 18.1 %bitcast_reduce_fusion = (f32[512,3]{0,1:T(4,128)S(1)}, f32[3,8192,512]{2,1,0:T(8,128)}) fusion(bf16[8192,3,128]{0,2,1:T(8,128)(2,1)S(1)} %bitcast.38, bf16[512,3,64]{2,0,1:T(8,128)(2,1)S(1)} %get-tuple-element.16, bf16[512,3,64]{2,0,1:T(8,128)(2,1)S(1)} %get-tuple-element.15), kind=kOutput, calls=%fused_computation.1 | convolution fusion | flops 3247176192 | bytes 57022464 | tf_op jit(solution)/shard_map/qhd,khd->qhk/dot_general | solution.py:63
  201.7 22.2 %fusion.1 = f32[512,3]{0,1:T(4,128)S(1)} fusion(f32[3,8192,512]{2,1,0:T(8,128)} %get-tuple-element.27, f32[512,3]{0,1:T(4,128)S(1)} %get-tuple-element.26), kind=kLoop, calls=%fused_computation.3 | loop fusion | flops 37747200 | bytes 50343936 | tf_op jit(solution)/shard_map/reduce_sum | solution.py:68
  224.0 17.9 %divide_convert_fusion = bf16[512,3,128]{0,2,1:T(8,128)(2,1)S(1)} fusion(bf16[8192,3,128]{0,2,1:T(8,128)(2,1)S(1)} %bitcast.40, f32[3,8192,512]{2,1,0:T(8,128)} %get-tuple-element.27, f32[512,3]{0,1:T(4,128)S(1)} %get-tuple-element.26, f32[512,3]{0,1:T(4,128)S(1)} %fusion.1), kind=kOutput, calls=%fused_computation.25 | convolution fusion | flops 3259367424 | bytes 57028608 | tf_op jit(solution)/shard_map/qhk,khd->qhd/dot_general | solution.py:69
  241.9 6.8 %convolution_convert_fusion = bf16[512,5120]{1,0:T(8,128)(2,1)} fusion(bf16[512,384]{0,1:T(8,128)(2,1)S(1)} %bitcast.45, bf16[384,5120]{1,0:T(8,128)(2,1)} %param.12), kind=kOutput, calls=%fused_computation.14 | convolution fusion | flops 2015887360 | bytes 9568256 | tf_op jit(solution)/shard_map/dot_general | solution.py:74
  248.7 8.0 %copy.32 = bf16[512,5120]{0,1:T(8,128)(2,1)} copy(bf16[512,5120]{1,0:T(8,128)(2,1)} %convolution_convert_fusion) | data formatting | bytes 10485760
  256.8 60.0 %reduce-scatter.4.cloned.1.call-done = bf16[640,512]{1,0:T(8,128)(2,1)} async-done(((bf16[5120,512]{1,0:T(8,128)(2,1)}), bf16[640,512]{1,0:T(8,128)(2,1)}) %reduce-scatter.4.cloned.1.call-update) | async-done | bytes 655376
  316.8 1.4 copy.33
  318.2 1.0 add_convert_fusion
  (25 shorter events, 2.1 us)
Async XLA Ops:
  6.5 68.1 %all-gather.5.cloned.1.call-start = ((), (), s32[]{:S(2)}) async-start(), calls=%async_computation.2 | async-start | bytes 5898240 | tf_op jit(solution)/shard_map/all_gather | solution.py:28
  7.3 167.1 %all-gather.3.cloned.1.call-start = ((), (), s32[]{:S(2)}) async-start(), calls=%async_computation.1 | async-start | bytes 13369344 | tf_op jit(solution)/shard_map/all_gather | solution.py:55
  10.4 306.4 %reduce-scatter.4.cloned.1.call-start = ((), (), s32[]{:S(2)}) async-start(), calls=%async_computation.3 | async-start | bytes 5898240
  74.7 7.4 %copy-start = (bf16[512,5120]{1,0:T(8,128)(2,1)S(1)}, bf16[512,5120]{1,0:T(8,128)(2,1)}, u32[]{:S(2)}) copy-start(bf16[512,5120]{1,0:T(8,128)(2,1)} %all-gather.5.cloned.1.call-done) | copy-start | bytes 15728644
  93.6 1.4 copy-start.3
  201.7 22.3 %copy-start.1 = (bf16[8192,1,384]{0,2,1:T(8,128)(2,1)S(1)}, bf16[8192,1,384]{0,2,1:T(8,128)(2,1)}, u32[]{:S(2)}) copy-start(bf16[8192,1,384]{0,2,1:T(8,128)(2,1)} %get-tuple-element.12) | copy-start | bytes 18874372
  248.7 69.4 %copy-start.2 = (bf16[512,640]{1,0:T(8,128)(2,1)S(1)}, bf16[512,640]{1,0:T(8,128)(2,1)}, u32[]{:S(2)}) copy-start(bf16[512,640]{1,0:T(8,128)(2,1)} %param.7) | copy-start | bytes 1966084
Sparse Core Ops, SparseCore 0:
  9.0 65.6 all-gather.4
  77.0 97.3 all-gather.2
  256.9 59.8 reduce-scatter.3
where the time goes:
time: 327 us; the launch traced here: 326 us
  waiting for transfers between devices  183 us (56%)
  matrix products  54.4 us (17%)
  other arithmetic  39 us (12%)
  local copies, waits for them, and re-layouts  23.6 us (7%)
  between operations  13.2 us (4%)
  blocking collectives  12.8 us (4%)
    all_gather x1, waiting for transfers between devices, local(): stale_all = lax.all_gather(stale_kv, 'patch', axis=0, tiled=True)  62 us
    unnamed x4, waiting for transfers between devices  60.7 us
    all_gather x1, waiting for transfers between devices, local(): gathered_in = lax.all_gather(hidden_in, 'head', axis=1, tiled=True)  59.9 us
    reduce_sum x1, other arithmetic, local(): totals = jnp.sum(weights, axis=-1)  22.2 us
    dot_general x1, matrix products, local(): jnp.einsum('qhd,khd->qhk', rotated_queries, key_rows, preferred_element_t...  18.1 us
    dot_general x1, matrix products, local(): jnp.einsum('qhk,khd->qhd', weights.astype(jnp.bfloat16), value_rows, pref...  17.9 us
    unnamed x11, local copies, waits for them, and re-layouts  13.9 us
    psum x1, blocking collectives, local(): lax.psum((jnp.sum(queries * queries, axis=-1), jnp.sum(keys_new * keys_ne...  12.8 us
  transfers between devices with their start and end apart: 3, of which 3 were waited for; matrix products, arithmetic and copies ran while one was open for 9% of the time, Pallas kernels for 0%

commit v1 on v0

v1 whole, which is shorter than its diff:
```python
import functools
import math

import jax
import jax.numpy as jnp
from jax import lax
from jax.experimental import pallas as pl
from jax.experimental.pallas import tpu as pltpu
from jax.sharding import PartitionSpec as P

HD = 128
HEADS_DEV = 3
MODEL = 5120
COLS = 640
ROWS = 512
WIDTH = 384
FULL = 3072
TILE = 256
EXP_SCALE = HD ** (-0.5) * math.log2(math.e)
MESH = pl.DeviceIdType.MESH
NT = (((1,), (1,)), ((), ()))
PEERS = (6, 2, 5, 7, 1, 3, 4)


def dot(left, right):
    return jnp.dot(left, right, preferred_element_type=jnp.float32)


def dot_nt(left, right):
    return lax.dot_general(left, right, NT, preferred_element_type=jnp.float32)


def mirrored(rel):
    return 4 * (rel // 4) + (4 - rel % 4) % 4


def to_rows(columns):
    lane = lax.broadcasted_iota(jnp.int32, (ROWS, 128), 1)
    wide = jnp.where(lane == 0, columns[0], jnp.where(lane == 1, columns[1], 0.0))
    return wide.T[:8]


def to_columns(first, second):
    sub = lax.broadcasted_iota(jnp.int32, (128, ROWS), 0)
    tall = jnp.where(sub == 0, first, jnp.where(sub == 1, second, 0.0)).T
    return (
        jnp.broadcast_to(tall[:, 0:1], (ROWS, 128)),
        jnp.broadcast_to(tall[:, 1:2], (ROWS, 128)),
    )


def kernel(
    hid_in, ang, modulation, w_in, gain, wout_in, kv_in, out,
    hid, w, kv, wo, att, acc, q, cosine, sine, mean, rstd, stats, norms,
    own_stats, own_norms, run_max, run_sum, run_acc, score, total, send, recv, local,
):
    patch, head = lax.axis_index("patch"), lax.axis_index("head")
    z, xh, core = patch // 4, (patch // 2) % 2, patch % 2
    xl, y = head // 4, head % 4
    count = [0]
    copies = []

    def place(dz=0, dxh=0, dcore=0, rel=0):
        to_patch = ((z + dz) % 4) * 4 + ((xh + dxh) % 2) * 2 + (core + dcore) % 2
        to_head = ((xl + rel // 4) % 2) * 4 + (y + rel % 4) % 4
        return (to_patch, to_head)

    def ship(src, dst, to):
        i = count[0]
        count[0] += 1
        copy = pltpu.make_async_remote_copy(
            src_ref=src, dst_ref=dst, send_sem=send.at[i], recv_sem=recv.at[i],
            device_id=to, device_id_type=MESH,
        )
        copy.start()
        copies.append(copy)
        return copy

    load_hid = pltpu.make_async_copy(hid_in, hid.at[0], local.at[0])
    load_hid.start()
    load_w = pltpu.make_async_copy(w_in, w, local.at[1])
    load_w.start()
    own_cols = pl.ds(pl.multiple_of(head * COLS, COLS), COLS)
    load_wo = pltpu.make_async_copy(wout_in.at[:, own_cols], wo.at[0], local.at[2])
    load_wo.start()

    partners = [place(rel=r) for r in PEERS]
    partners += [place(dz=1), place(dz=3), place(dxh=1), place(dcore=1)]
    barrier = pltpu.get_barrier_semaphore()
    for to in partners:
        pl.semaphore_signal(barrier, inc=1, device_id=to, device_id_type=MESH)
    pl.semaphore_wait(barrier, len(partners))

    part = lambda t: pl.ds(t * TILE, TILE)
    near = {}
    for t in range(2):
        for rel in (1, 3, 4):
            near[rel, t] = ship(
                hid_in.at[part(t)], hid.at[mirrored(rel), part(t)], place(rel=rel)
            )
    kv_own = {
        dz: ship(kv_in, kv.at[((4 - dz) % 4) * 4], place(dz=dz)) for dz in (1, 3)
    }
    kv_core = [ship(kv_in, kv.at[1], place(dcore=1))]

    def pass_to_core(slot):
        kv_core.append(ship(kv.at[slot], kv.at[slot + 1], place(dcore=1)))

    load_hid.wait()
    own = hid[0].astype(jnp.float32)
    own_sum = jnp.sum(own, axis=1, keepdims=True)
    off = own - own_sum * (1.0 / COLS)
    own_stats[...] = to_rows((own_sum, jnp.sum(off * off, axis=1, keepdims=True)))
    stat_copies = [
        ship(own_stats, stats.at[mirrored(r)], place(rel=r)) for r in PEERS
    ]
    stats[0] = own_stats[...]

    angles = ang[...]
    lane = lax.broadcasted_iota(jnp.int32, (ROWS, HD), 1)
    cosine[...] = jnp.cos(angles)
    sine[...] = jnp.where(lane < HD // 2, -1.0, 1.0) * jnp.sin(angles)

    for copy in stat_copies:
        copy.wait_recv()
    sums = sum(stats[r, 0:1, :] for r in range(8))
    mean_row = sums * (1.0 / MODEL)
    squares = sum(
        stats[r, 1:2, :] + COLS * jnp.square(stats[r, 0:1, :] * (1.0 / COLS) - mean_row)
        for r in range(8)
    )
    mean[...], rstd[...] = to_columns(mean_row, lax.rsqrt(squares * (1.0 / MODEL) + 1e-6))
    load_w.wait()

    def project(rel, t, first=False):
        rows = slice(t * TILE, t * TILE + TILE)
        block = ((xl + rel // 4) % 2) * 4 + (y + rel % 4) % 4
        at = pl.ds(pl.multiple_of(block * COLS, COLS), COLS)
        features = hid[rel, rows].astype(jnp.float32)
        centre = jnp.concatenate([mean[rows]] * (COLS // 128), axis=1)
        factor = jnp.concatenate([rstd[rows]] * (COLS // 128), axis=1)
        shift, scale = modulation[0:1, at], modulation[1:2, at]
        modulated = ((features - centre) * factor * (1.0 + scale) + shift).astype(jnp.bfloat16)
        for j in range(3):
            cols = slice(j * WIDTH, j * WIDTH + WIDTH)
            term = dot(modulated, w[j, at, :])
            if first:
                acc[rows, cols] = term
            else:
                acc[rows, cols] += term

    for t in range(2):
        project(0, t, first=True)

    QUARTER = TILE // 2
    far, fwd, opp = {}, {}, {}
    for t in range(2):
        near[1, t].wait_recv()
        near[3, t].wait_recv()
        low, high = pl.ds(t * TILE, QUARTER), pl.ds(t * TILE + QUARTER, QUARTER)
        far[t] = (
            ship(hid.at[3, low], hid.at[2, low], place(rel=1)),
            ship(hid.at[1, high], hid.at[2, high], place(rel=3)),
        )
        near[4, t].wait_recv()
        fwd[t] = (
            ship(hid.at[4, part(t)], hid.at[7, part(t)], place(rel=1)),
            ship(hid.at[4, part(t)], hid.at[5, part(t)], place(rel=3)),
        )
        if t == 1:
            kv_x = ship(kv_in, kv.at[2], place(dxh=1))
        for rel in (1, 3, 4):
            project(rel, t)
    kv_own[1].wait_recv()
    kv_own[3].wait_recv()
    kv_far = [
        ship(kv.at[12, 0], kv.at[8, 0], place(dz=1)),
        ship(kv.at[4, 1], kv.at[8, 1], place(dz=3)),
    ]
    pass_to_core(12)
    pass_to_core(4)
    for t in range(2):
        for copy in far[t]:
            copy.wait_recv()
        opp[t] = ship(hid.at[2, part(t)], hid.at[6, part(t)], place(rel=4))
        project(2, t)
    for copy in fwd[0]:
        copy.wait_recv()
    project(5, 0)
    project(7, 0)
    kv_x.wait_recv()
    kv_x_own = [
        ship(kv.at[2], kv.at[14], place(dz=1)),
        ship(kv.at[2], kv.at[6], place(dz=3)),
    ]
    pass_to_core(2)
    for copy in fwd[1]:
        copy.wait_recv()
    project(5, 1)
    project(7, 1)
    for t in range(2):
        opp[t].wait_recv()
        project(6, t)

    queries, keys = acc[:, :WIDTH], acc[:, WIDTH : 2 * WIDTH]
    own_norms[...] = to_rows(
        (
            jnp.sum(queries * queries, axis=1, keepdims=True),
            jnp.sum(keys * keys, axis=1, keepdims=True),
        )
    )
    norm_copies = [
        ship(own_norms, norms.at[mirrored(r)], place(rel=r)) for r in PEERS
    ]
    norms[0] = own_norms[...]
    half = pl.ds(pl.multiple_of(core * (WIDTH // 2), WIDTH // 2), WIDTH // 2)
    wo_copies = {}
    for r in PEERS:
        to = place(rel=r)
        cols = pl.ds(pl.multiple_of(to[1] * COLS, COLS), COLS)
        wo_copies[mirrored(r)] = ship(wout_in.at[half, cols], wo.at[mirrored(r), half], to)
    kv[0, 1] = acc[:, 2 * WIDTH :].astype(jnp.bfloat16)
    for copy in norm_copies:
        copy.wait_recv()
    q_row, k_row = (
        lax.rsqrt(sum(norms[r, i : i + 1, :] for r in range(8)) * (1.0 / FULL) + 1e-6)
        for i in range(2)
    )
    q_factor, k_factor = to_columns(q_row, k_row)
    for h in range(HEADS_DEV):
        for i, factor in ((0, q_factor), (1, k_factor)):
            cols = slice(h * HD, h * HD + HD)
            value = acc[:, i * WIDTH + h * HD : i * WIDTH + h * HD + HD] * factor * gain[i : i + 1, cols]
            turned = (
                value * cosine[...] + pltpu.roll(value, HD // 2, 1) * sine[...]
            ).astype(jnp.bfloat16)
            if i == 0:
                q[h] = turned
            else:
                kv[0, 0, :, cols] = turned

    for copy in kv_far:
        copy.wait_recv()
    pass_to_core(8)
    for copy in kv_x_own:
        copy.wait_recv()
    kv_x_far = [
        ship(kv.at[14, 0], kv.at[10, 0], place(dz=1)),
        ship(kv.at[6, 1], kv.at[10, 1], place(dz=3)),
    ]
    pass_to_core(14)
    pass_to_core(6)
    for copy in kv_x_far:
        copy.wait_recv()
    pass_to_core(10)
    for copy in kv_core:
        copy.wait_recv()

    att_copies = []
    wo_core = {}
    for h in range(HEADS_DEV):
        cols = slice(h * HD, h * HD + HD)
        run_max[...] = jnp.full_like(run_max, -1e30)
        run_sum[...] = jnp.zeros_like(run_sum)
        run_acc[...] = jnp.zeros_like(run_acc)
        for t in range(2):
            rows = slice(t * TILE, t * TILE + TILE)
            score[0, rows] = dot_nt(q[h, rows], kv[0, 0, :, cols])

        def body(i, carry):
            for u in range(2):
                slot = 2 * i + u
                after = jnp.minimum(slot + 1, 15)
                for t in range(2):
                    rows = slice(t * TILE, t * TILE + TILE)
                    score[1 - u, rows] = dot_nt(q[h, rows], kv[after, 0, :, cols])
                    now = score[u, rows]
                    high = now[:, :128]
                    for g in range(1, 4):
                        high = jnp.maximum(high, now[:, g * 128 : g * 128 + 128])
                    old = run_max[rows]
                    new = jnp.maximum(old, jnp.max(high, axis=1, keepdims=True))
                    fade = jnp.exp2((old - new) * EXP_SCALE)
                    tally = run_sum[rows] * fade
                    pieces = []
                    for g in range(4):
                        weight = jnp.exp2((now[:, g * 128 : g * 128 + 128] - new) * EXP_SCALE)
                        tally = tally + weight
                        pieces.append(weight.astype(jnp.bfloat16))
                    weights = jnp.concatenate(pieces, axis=1)
                    run_acc[rows] = run_acc[rows] * fade + dot(weights, kv[slot, 1, :, cols])
                    run_max[rows] = new
                    run_sum[rows] = tally
            return carry

        lax.fori_loop(0, 8, body, 0)
        att[0, :, cols] = (
            run_acc[...] / jnp.sum(run_sum[...], axis=1, keepdims=True)
        ).astype(jnp.bfloat16)
        for r in PEERS:
            att_copies.append(
                (mirrored(r), ship(att.at[0, :, cols], att.at[mirrored(r), :, cols], place(rel=r)))
            )
        if h == 0:
            for r in PEERS:
                wo_copies[r].wait_recv()
                wo_core[r] = ship(wo.at[r, half], wo.at[r, half], place(dcore=1))

    load_wo.wait()
    for r in (0,) + PEERS[::-1]:
        if r:
            for rel, copy in att_copies:
                if rel == r:
                    copy.wait_recv()
            wo_core[r].wait_recv()
        for t in range(2):
            rows = slice(t * TILE, t * TILE + TILE)
            term = dot(att[r, rows], wo[r]).astype(jnp.bfloat16).astype(jnp.float32)
            if r == 0:
                total[rows] = term
            else:
                total[rows] += term
    gate = modulation[2:3, own_cols]
    out[...] = (hid[0].astype(jnp.float32) + gate * total[...]).astype(jnp.bfloat16)
    for copy in copies:
        copy.wait_send()


def local(hidden_in, positions, modulation, w_qkv, qk_gain, w_out, stale_kv):
    half_dim = HD // 2
    inverse_freq = 10000.0 ** (-2.0 * jnp.arange(half_dim, dtype=jnp.float32) / HD)
    angles = positions.astype(jnp.float32)[:, None] * jnp.concatenate([inverse_freq] * 2)[None, :]
    vmem = pl.BlockSpec(memory_space=pltpu.VMEM)
    hbm = pl.BlockSpec(memory_space=pl.ANY)
    f32, bf16 = jnp.float32, jnp.bfloat16
    copies = 100
    return pl.pallas_call(
        kernel,
        out_shape=jax.ShapeDtypeStruct((ROWS, COLS), bf16),
        in_specs=[hbm, vmem, vmem, hbm, vmem, hbm, hbm],
        out_specs=vmem,
        scratch_shapes=[
            pltpu.VMEM((8, ROWS, COLS), bf16),
            pltpu.VMEM((3, MODEL, WIDTH), bf16),
            pltpu.VMEM((16, 2, ROWS, WIDTH), bf16),
            pltpu.VMEM((8, WIDTH, COLS), bf16),
            pltpu.VMEM((8, ROWS, WIDTH), bf16),
            pltpu.VMEM((ROWS, 3 * WIDTH), f32),
            pltpu.VMEM((HEADS_DEV, ROWS, HD), bf16),
            pltpu.VMEM((ROWS, HD), f32),
            pltpu.VMEM((ROWS, HD), f32),
            pltpu.VMEM((ROWS, 128), f32),
            pltpu.VMEM((ROWS, 128), f32),
            pltpu.VMEM((8, 8, ROWS), f32),
            pltpu.VMEM((8, 8, ROWS), f32),
            pltpu.VMEM((8, ROWS), f32),
            pltpu.VMEM((8, ROWS), f32),
            pltpu.VMEM((ROWS, 128), f32),
            pltpu.VMEM((ROWS, 128), f32),
            pltpu.VMEM((ROWS, HD), f32),
            pltpu.VMEM((2, ROWS, ROWS), f32),
            pltpu.VMEM((ROWS, COLS), f32),
            pltpu.SemaphoreType.DMA((copies,)),
            pltpu.SemaphoreType.DMA((copies,)),
            pltpu.SemaphoreType.DMA((3,)),
        ],
        compiler_params=pltpu.CompilerParams(
            collective_id=0, has_side_effects=True, vmem_limit_bytes=60 << 20
        ),
        cost_estimate=pl.CostEstimate(
            flops=15_000_000_000, bytes_accessed=40_000_000, transcendentals=13_000_000
        ),
        name="attention_sublayer",
    )(
        hidden_in, angles, modulation, jnp.transpose(w_qkv, (1, 0, 2)), qk_gain, w_out,
        jnp.transpose(stale_kv, (1, 0, 2)),
    )


def solution(mesh):
    return jax.shard_map(
        local,
        mesh=mesh,
        in_specs=(
            P("patch", "head"),
            P("patch"),
            P(),
            P(None, None, "head"),
            P(None, "head"),
            P("head", None),
            P("patch", None, "head"),
        ),
        out_specs=P("patch", "head"),
        check_vma=False,
    )
```

time: 327 us -> 144 us (0.44)
  waiting for transfers between devices: 183 us -> 0 us
  Pallas kernels: 0 us -> 138 us
  matrix products: 54.4 us -> 0 us
  other arithmetic: 39 us -> 1.62 us
  local copies, waits for them, and re-layouts: 23.6 us -> 4.09 us
  between operations: 13.2 us -> 0.01 us
  blocking collectives: 12.8 us -> 0 us
    pallas_call x0 -> x1, Pallas kernels: none -> 138 us  [local(): pl.pallas_call(kernel, out_shape=jax.ShapeDtypeStruct((ROWS, COLS), bf16)...]
    all_gather x2 -> x0, waiting for transfers between devices: 122 us -> none  [the longest x1 62 us: local(): stale_all = lax.all_gather(stale_kv, 'patch', axis=0, tiled=True)]
    unnamed x4 -> x0, waiting for transfers between devices: 60.7 us -> none
    dot_general x4 -> x0, matrix products: 54.4 us -> none  [the longest x1 18.1 us: local(): jnp.einsum('qhd,khd->qhk', rotated_queries, key_rows, preferred_element_t...]
    reduce_sum x4 -> x0, other arithmetic: 31.3 us -> none  [the longest x1 22.2 us: local(): totals = jnp.sum(weights, axis=-1)]
    psum x1 -> x0, blocking collectives: 12.8 us -> none  [local(): lax.psum((jnp.sum(queries * queries, axis=-1), jnp.sum(keys_new * keys_ne...]
    unnamed x11 -> x2, local copies, waits for them, and re-layouts: 13.9 us -> 4.09 us
    slice x3 -> x0, local copies, waits for them, and re-layouts: 9.02 us -> none  [the longest x1 8.19 us: local(): key_rows = merged_rows[:, 0].reshape(-1, head_count, HD)]
  transfers between devices with their start and end apart: 3 -> 0, of which waited for: 3 -> 0; matrix products, arithmetic and copies ran while one was open for 9% -> 0% of each run, Pallas kernels for 0% -> 0%
where the time goes in v1:
time: 144 us; the launch traced here: 143 us
  Pallas kernels  138 us (96%)
  local copies, waits for them, and re-layouts  4.09 us (3%)
  other arithmetic  1.62 us (1%)
    pallas_call x1, Pallas kernels, local(): pl.pallas_call(kernel, out_shape=jax.ShapeDtypeStruct((ROWS, COLS), bf16)...  138 us
    unnamed x2, local copies, waits for them, and re-layouts  4.09 us

profile of v1, /device:TPU:1, one launch (start us, length us, event | category | flops | bytes accessed | tf_op | source)
XLA Modules:
  0.0 143.4 jit_solution(7799138330178656493)
XLA Ops:
  0.0 0.1 pad_maximum_fusion
  0.1 0.7 convert_element_type.3
  0.8 0.8 broadcast_multiply_fusion.ang
  1.6 2.1 %copy.10 = bf16[512,2,384]{2,0,1:T(8,128)(2,1)} copy(bf16[512,2,384]{2,1,0:T(2,128)(2,1)} %param.13) | data formatting | bytes 1572864 | tf_op args[6]
  3.7 137.7 %attention_sublayer.1 = bf16[512,640]{1,0:T(8,128)(2,1)} custom-call(bf16[512,640]{1,0:T(8,128)(2,1)} %hid_in.1, f32[512,128]{1,0:T(8,128)} %broadcast_multiply_fusion.ang, f32[3,5120]{1,0:T(4,128)} %modulation.1, bf16[3,5120,384]{2,1,0:T(8,128)(2,1)} %bitcast.5, f32[2,384]{1,0:T(2,128)} %gain.1, bf16[384,5120]{1,0:T(8,128)(2,1)} %wout_in.1, ...), custom_call_target="tpu_custom_call" | custom-call | flops 15000000512 | bytes 40000000 | tf_op jit(solution)/shard_map/attention_sublayer/pallas_call | solution.py:337
  141.4 2.0 %copy.12 = bf16[512,640]{1,0:T(8,128)(2,1)} copy(bf16[512,640]{1,0:T(8,128)(2,1)} %attention_sublayer.1) | data formatting | bytes 1310720
  (1 shorter events, 0.0 us)

commit v2 on v1

v2 whole, which is shorter than its diff:
```python
import functools
import math

import jax
import jax.numpy as jnp
from jax import lax
from jax.experimental import pallas as pl
from jax.experimental.pallas import tpu as pltpu
from jax.sharding import PartitionSpec as P

HD = 128
HEADS_DEV = 3
MODEL = 5120
COLS = 640
ROWS = 512
WIDTH = 384
FULL = 3072
TILE = 256
EXP_SCALE = HD ** (-0.5) * math.log2(math.e)
MESH = pl.DeviceIdType.MESH
NT = (((1,), (1,)), ((), ()))
PEERS = (6, 2, 5, 7, 1, 3, 4)
WO_SLOT = (0, 1, 4, 2, 3, 5, 6, 7)
ORDER = (
    (0, 0, 1), (1, 0, 0), (1, 0, 1), (3, 0, 0), (3, 0, 1), (2, 0, 0), (2, 0, 1), (0, 1, 0),
    (0, 1, 1), (1, 1, 0), (1, 1, 1), (3, 1, 0), (3, 1, 1), (2, 1, 0), (2, 1, 1), (0, 0, 0),
)
SLOT = {where: i for i, where in enumerate(ORDER)}
OWN = SLOT[0, 0, 0]


def dot(left, right):
    return jnp.dot(left, right, preferred_element_type=jnp.float32)


def dot_nt(left, right):
    return lax.dot_general(left, right, NT, preferred_element_type=jnp.float32)


def mirrored(rel):
    return 4 * (rel // 4) + (4 - rel % 4) % 4


def to_rows(first, second):
    lane = lax.broadcasted_iota(jnp.int32, (first.shape[0], 128), 1)
    wide = jnp.where(lane == 0, first, jnp.where(lane == 1, second, 0.0))
    return wide.T[:8]


def to_columns(first, second):
    n = first.shape[1]
    sub = lax.broadcasted_iota(jnp.int32, (128, n), 0)
    tall = jnp.where(sub == 0, first, jnp.where(sub == 1, second, 0.0)).T
    return (
        jnp.broadcast_to(tall[:, 0:1], (n, 128)),
        jnp.broadcast_to(tall[:, 1:2], (n, 128)),
    )


def kernel(
    hid_in, places, freq, modulation, w_in, gain, wout_in, kv_in, out,
    hid, w, kv, wo, att, acc, q, cosine, sine, mean, rstd, stats, norms,
    own_stats, own_norms, run_max, run_sum, run_acc, score, total, send, recv, local,
):
    patch, head = lax.axis_index("patch"), lax.axis_index("head")
    z, xh, core = patch // 4, (patch // 2) % 2, patch % 2
    xl, y = head // 4, head % 4
    count = [0]
    copies = []

    def place(dz=0, dxh=0, dcore=0, rel=0):
        to_patch = ((z + dz) % 4) * 4 + ((xh + dxh) % 2) * 2 + (core + dcore) % 2
        to_head = ((xl + rel // 4) % 2) * 4 + (y + rel % 4) % 4
        return (to_patch, to_head)

    def ship(src, dst, to):
        i = count[0]
        count[0] += 1
        copy = pltpu.make_async_remote_copy(
            src_ref=src, dst_ref=dst, send_sem=send.at[i], recv_sem=recv.at[i],
            device_id=to, device_id_type=MESH,
        )
        copy.start()
        copies.append(copy)
        return copy

    def arrive(*these):
        for copy in these:
            copy.wait_recv()

    load_hid = pltpu.make_async_copy(hid_in, hid.at[0], local.at[0])
    load_hid.start()
    load_w = pltpu.make_async_copy(w_in, w, local.at[1])
    load_w.start()
    own_cols = pl.ds(pl.multiple_of(head * COLS, COLS), COLS)
    load_wo = pltpu.make_async_copy(wout_in.at[:, own_cols], wo.at[0], local.at[2])
    load_wo.start()

    partners = [place(rel=r) for r in PEERS]
    partners += [place(dz=1), place(dz=3), place(dxh=1), place(dcore=1)]
    barrier = pltpu.get_barrier_semaphore()
    for to in partners:
        pl.semaphore_signal(barrier, inc=1, device_id=to, device_id_type=MESH)
    pl.semaphore_wait(barrier, len(partners))

    part = lambda t: pl.ds(t * TILE, TILE)
    low = lambda t: pl.ds(t * TILE, TILE // 2)
    high = lambda t: pl.ds(t * TILE + TILE // 2, TILE // 2)

    def spread(buffer, source, t):
        return {
            rel: ship(source.at[part(t)], buffer.at[mirrored(rel), part(t)], place(rel=rel))
            for rel in (1, 3, 4)
        }

    def relay(buffer, near, t):
        arrive(near[1], near[3])
        far = (
            ship(buffer.at[3, low(t)], buffer.at[2, low(t)], place(rel=1)),
            ship(buffer.at[1, high(t)], buffer.at[2, high(t)], place(rel=3)),
        )
        arrive(near[4])
        side = (
            ship(buffer.at[4, part(t)], buffer.at[7, part(t)], place(rel=1)),
            ship(buffer.at[4, part(t)], buffer.at[5, part(t)], place(rel=3)),
        )
        return far, side

    def across_y(buffer, far, side, t):
        arrive(*far, *side)
        return (
            ship(buffer.at[7, low(t)], buffer.at[6, low(t)], place(rel=1)),
            ship(buffer.at[5, high(t)], buffer.at[6, high(t)], place(rel=3)),
        )

    def pass_to_core(where):
        here, there = SLOT[where + (0,)], SLOT[where + (1,)]
        return ship(kv.at[here], kv.at[there], place(dcore=1))

    near, far, side, opp = {}, {}, {}, {}
    near[0] = spread(hid, hid_in, 0)
    kv_z = {dz: ship(kv_in, kv.at[SLOT[(4 - dz) % 4, 0, 0]], place(dz=dz)) for dz in (1, 3)}
    kv_core = {(0, 0): ship(kv_in, kv.at[SLOT[0, 0, 1]], place(dcore=1))}

    load_hid.wait()
    own = hid[0].astype(jnp.float32)
    own_sum = jnp.sum(own, axis=1, keepdims=True)
    off = own - own_sum * (1.0 / COLS)
    own_stats[...] = to_rows(own_sum, jnp.sum(off * off, axis=1, keepdims=True))
    stat_copies = [ship(own_stats, stats.at[mirrored(r)], place(rel=r)) for r in PEERS]
    stats[0] = own_stats[...]

    spots = places[...].astype(jnp.float32)
    angles = to_columns(spots, spots)[0] * freq[...]
    lane = lax.broadcasted_iota(jnp.int32, (ROWS, HD), 1)
    cosine[...] = jnp.cos(angles)
    sine[...] = jnp.where(lane < HD // 2, -1.0, 1.0) * jnp.sin(angles)

    arrive(*stat_copies)
    sums = sum(stats[r, 0:1, :] for r in range(8))
    mean_row = sums * (1.0 / MODEL)
    squares = sum(
        stats[r, 1:2, :] + COLS * jnp.square(stats[r, 0:1, :] * (1.0 / COLS) - mean_row)
        for r in range(8)
    )
    mean[...], rstd[...] = to_columns(mean_row, lax.rsqrt(squares * (1.0 / MODEL) + 1e-6))
    load_w.wait()

    def project(rel, t):
        rows = slice(t * TILE, t * TILE + TILE)
        block = ((xl + rel // 4) % 2) * 4 + (y + rel % 4) % 4
        at = pl.ds(pl.multiple_of(block * COLS, COLS), COLS)
        features = hid[rel, rows].astype(jnp.float32)
        centre = jnp.concatenate([mean[rows]] * (COLS // 128), axis=1)
        factor = jnp.concatenate([rstd[rows]] * (COLS // 128), axis=1)
        shift, scale = modulation[0:1, at], modulation[1:2, at]
        modulated = ((features - centre) * factor * (1.0 + scale) + shift).astype(jnp.bfloat16)
        for j in range(3):
            cols = slice(j * WIDTH, j * WIDTH + WIDTH)
            term = dot(modulated, w[j, at, :])
            if rel == 0:
                acc[rows, cols] = term
            else:
                acc[rows, cols] += term

    def send_norms(t):
        rows = slice(t * TILE, t * TILE + TILE)
        queries, keys = acc[rows, :WIDTH], acc[rows, WIDTH : 2 * WIDTH]
        own_norms[t] = to_rows(
            jnp.sum(queries * queries, axis=1, keepdims=True),
            jnp.sum(keys * keys, axis=1, keepdims=True),
        )
        norms[t, 0] = own_norms[t]
        return [ship(own_norms.at[t], norms.at[t, mirrored(r)], place(rel=r)) for r in PEERS]

    def finish_projection(t, norm_copies):
        rows = slice(t * TILE, t * TILE + TILE)
        kv[OWN, 1, rows] = acc[rows, 2 * WIDTH :].astype(jnp.bfloat16)
        arrive(*norm_copies)
        factors = to_columns(
            *(
                lax.rsqrt(sum(norms[t, r, i : i + 1, :] for r in range(8)) * (1.0 / FULL) + 1e-6)
                for i in range(2)
            )
        )
        for h in range(HEADS_DEV):
            for i, factor in enumerate(factors):
                cols = slice(h * HD, h * HD + HD)
                value = acc[rows, i * WIDTH + h * HD : i * WIDTH + h * HD + HD]
                value = value * factor * gain[i : i + 1, cols]
                turned = value * cosine[rows] + pltpu.roll(value, HD // 2, 1) * sine[rows]
                if i == 0:
                    q[h, rows] = turned.astype(jnp.bfloat16)
                else:
                    kv[OWN, 0, rows, cols] = turned.astype(jnp.bfloat16)

    def attend(t, first, slots):
        rows = slice(t * TILE, t * TILE + TILE)
        columns = [slice(h * HD, h * HD + HD) for h in range(HEADS_DEV)]
        for h, cols in enumerate(columns):
            if first == 0:
                run_max[h, rows] = jnp.full((TILE, 128), -1e30, jnp.float32)
                run_sum[h, rows] = jnp.zeros((TILE, 128), jnp.float32)
                run_acc[h, rows] = jnp.zeros((TILE, HD), jnp.float32)
            score[0, h] = dot_nt(q[h, rows], kv[first, 0, :, cols])

        def body(i, carry):
            for u in range(2):
                slot = first + 2 * i + u
                after = jnp.minimum(slot + 1, first + slots - 1)
                for h, cols in enumerate(columns):
                    score[1 - u, h] = dot_nt(q[h, rows], kv[after, 0, :, cols])
                    now = score[u, h]
                    peak = now[:, :128]
                    for g in range(1, 4):
                        peak = jnp.maximum(peak, now[:, g * 128 : g * 128 + 128])
                    old = run_max[h, rows]
                    new = jnp.maximum(old, jnp.max(peak, axis=1, keepdims=True))
                    fade = jnp.exp2((old - new) * EXP_SCALE)
                    tally = run_sum[h, rows] * fade
                    pieces = []
                    for g in range(4):
                        weight = jnp.exp2((now[:, g * 128 : g * 128 + 128] - new) * EXP_SCALE)
                        tally = tally + weight
                        pieces.append(weight.astype(jnp.bfloat16))
                    weights = jnp.concatenate(pieces, axis=1)
                    run_acc[h, rows] = run_acc[h, rows] * fade + dot(weights, kv[slot, 1, :, cols])
                    run_max[h, rows] = new
                    run_sum[h, rows] = tally
            return carry

        lax.fori_loop(0, slots // 2, body, 0)

    def publish(t):
        rows = slice(t * TILE, t * TILE + TILE)
        for h in range(HEADS_DEV):
            att[0, rows, h * HD : h * HD + HD] = (
                run_acc[h, rows] / jnp.sum(run_sum[h, rows], axis=1, keepdims=True)
            ).astype(jnp.bfloat16)
        return spread(att, att.at[0], t)

    def across_x(far, t):
        arrive(*far)
        return ship(att.at[2, part(t)], att.at[6, part(t)], place(rel=4))

    def output(r, t):
        rows = slice(t * TILE, t * TILE + TILE)
        term = dot(att[r, rows], wo[WO_SLOT[r]]).astype(jnp.bfloat16).astype(jnp.float32)
        if r == 0:
            total[rows] = term
        else:
            total[rows] += term

    for t in range(2):
        project(0, t)
    far[0], side[0] = relay(hid, near[0], 0)
    kv_x = ship(kv_in, kv.at[SLOT[0, 1, 0]], place(dxh=1))
    for rel in (1, 3, 4):
        project(rel, 0)
    arrive(kv_z[1], kv_z[3])
    up, down, two = SLOT[3, 0, 0], SLOT[1, 0, 0], SLOT[2, 0, 0]
    kv_far = (
        ship(kv.at[up, 0], kv.at[two, 0], place(dz=1)),
        ship(kv.at[down, 1], kv.at[two, 1], place(dz=3)),
    )
    kv_core[3, 0], kv_core[1, 0] = pass_to_core((3, 0)), pass_to_core((1, 0))
    opp[0] = across_y(hid, far[0], side[0], 0)
    for rel in (2, 5, 7):
        project(rel, 0)
    near[1] = spread(hid, hid_in, 1)
    arrive(*opp[0])
    project(6, 0)
    norm_copies = send_norms(0)
    arrive(*kv_far)
    kv_core[2, 0] = pass_to_core((2, 0))
    kv_x_far = ship(kv.at[two], kv.at[SLOT[2, 1, 0]], place(dxh=1))
    arrive(kv_x)
    beside = SLOT[0, 1, 0]
    kv_x_z = (
        ship(kv.at[beside], kv.at[SLOT[3, 1, 0]], place(dz=1)),
        ship(kv.at[beside], kv.at[SLOT[1, 1, 0]], place(dz=3)),
    )
    kv_core[0, 1] = pass_to_core((0, 1))
    finish_projection(0, norm_copies)
    far[1], side[1] = relay(hid, near[1], 1)
    for rel in (1, 3, 4):
        project(rel, 1)
    arrive(kv_core[0, 0], kv_core[1, 0], kv_core[3, 0], kv_core[2, 0])
    attend(0, 0, 8)
    opp[1] = across_y(hid, far[1], side[1], 1)
    for rel in (2, 5, 7):
        project(rel, 1)
    HALF, EIGHTH = WIDTH // 2, WIDTH // 8
    half = pl.ds(pl.multiple_of(core * HALF, HALF), HALF)
    share = lambda dz: pl.ds(
        pl.multiple_of((((z + dz) % 4) * 2 + core) * EIGHTH, EIGHTH), EIGHTH
    )
    arrive(*opp[1])
    project(6, 1)
    norm_copies = send_norms(1)
    wo_copies = []
    for r in PEERS:
        to = place(rel=r)
        rows = half if r in (1, 3, 4) else share(0)
        cols = pl.ds(pl.multiple_of(to[1] * COLS, COLS), COLS)
        wo_copies.append(ship(wout_in.at[rows, cols], wo.at[WO_SLOT[mirrored(r)], rows], to))
    arrive(*kv_x_z)
    kv_core[3, 1], kv_core[1, 1] = pass_to_core((3, 1)), pass_to_core((1, 1))
    arrive(kv_x_far)
    kv_core[2, 1] = pass_to_core((2, 1))
    finish_projection(1, norm_copies)
    attend(1, 0, 8)
    arrive(*wo_copies)
    wo_z = [ship(wo.at[4:8, share(0)], wo.at[4:8, share(0)], place(dz=dz)) for dz in (1, 3)]
    wo_core = [
        ship(wo.at[1:4, half], wo.at[1:4, half], place(dcore=1)),
        ship(wo.at[4:8, share(0)], wo.at[4:8, share(0)], place(dcore=1)),
    ]
    arrive(kv_core[0, 1], kv_core[1, 1], kv_core[3, 1], kv_core[2, 1])
    attend(0, 8, 8)
    att_near = {0: publish(0)}
    att_far, att_side, att_opp = {}, {}, {}
    attend(1, 8, 4)
    att_far[0], att_side[0] = relay(att, att_near[0], 0)
    arrive(*wo_z)
    wo_far = (
        ship(wo.at[4:6, share(3)], wo.at[4:6, share(3)], place(dz=1)),
        ship(wo.at[6:8, share(1)], wo.at[6:8, share(1)], place(dz=3)),
    )
    for dz in (1, 3):
        wo_core.append(ship(wo.at[4:8, share(dz)], wo.at[4:8, share(dz)], place(dcore=1)))
    attend(1, 12, 4)
    att_near[1] = publish(1)
    att_opp[0] = across_x(att_far[0], 0)
    arrive(*wo_far)
    wo_core.append(ship(wo.at[4:8, share(2)], wo.at[4:8, share(2)], place(dcore=1)))
    load_wo.wait()
    output(0, 0)
    output(0, 1)
    att_far[1], att_side[1] = relay(att, att_near[1], 1)
    arrive(*wo_core)
    for r in (1, 3, 4, 2):
        output(r, 0)
    att_opp[1] = across_x(att_far[1], 1)
    arrive(*att_side[0], att_opp[0])
    for r in (5, 7, 6):
        output(r, 0)
    for r in (1, 3, 4, 2):
        output(r, 1)
    arrive(*att_side[1])
    output(5, 1)
    output(7, 1)
    arrive(att_opp[1])
    output(6, 1)
    gate = modulation[2:3, own_cols]
    out[...] = (hid[0].astype(jnp.float32) + gate * total[...]).astype(jnp.bfloat16)
    for copy in copies:
        copy.wait_send()


def local(hidden_in, positions, modulation, w_qkv, qk_gain, w_out, stale_kv):
    half_dim = HD // 2
    inverse_freq = 10000.0 ** (-2.0 * jnp.arange(half_dim, dtype=jnp.float32) / HD)
    frequencies = jnp.concatenate([inverse_freq] * 2)[None, :]
    vmem = pl.BlockSpec(memory_space=pltpu.VMEM)
    hbm = pl.BlockSpec(memory_space=pl.ANY)
    f32, bf16 = jnp.float32, jnp.bfloat16
    copies = 100
    return pl.pallas_call(
        kernel,
        out_shape=jax.ShapeDtypeStruct((ROWS, COLS), bf16),
        in_specs=[hbm, vmem, vmem, vmem, hbm, vmem, hbm, hbm],
        out_specs=vmem,
        scratch_shapes=[
            pltpu.VMEM((8, ROWS, COLS), bf16),
            pltpu.VMEM((3, MODEL, WIDTH), bf16),
            pltpu.VMEM((16, 2, ROWS, WIDTH), bf16),
            pltpu.VMEM((8, WIDTH, COLS), bf16),
            pltpu.VMEM((8, ROWS, WIDTH), bf16),
            pltpu.VMEM((ROWS, 3 * WIDTH), f32),
            pltpu.VMEM((HEADS_DEV, ROWS, HD), bf16),
            pltpu.VMEM((ROWS, HD), f32),
            pltpu.VMEM((ROWS, HD), f32),
            pltpu.VMEM((ROWS, 128), f32),
            pltpu.VMEM((ROWS, 128), f32),
            pltpu.VMEM((8, 8, ROWS), f32),
            pltpu.VMEM((2, 8, 8, TILE), f32),
            pltpu.VMEM((8, ROWS), f32),
            pltpu.VMEM((2, 8, TILE), f32),
            pltpu.VMEM((HEADS_DEV, ROWS, 128), f32),
            pltpu.VMEM((HEADS_DEV, ROWS, 128), f32),
            pltpu.VMEM((HEADS_DEV, ROWS, HD), f32),
            pltpu.VMEM((2, HEADS_DEV, TILE, ROWS), f32),
            pltpu.VMEM((ROWS, COLS), f32),
            pltpu.SemaphoreType.DMA((copies,)),
            pltpu.SemaphoreType.DMA((copies,)),
            pltpu.SemaphoreType.DMA((3,)),
        ],
        compiler_params=pltpu.CompilerParams(
            collective_id=0, has_side_effects=True, vmem_limit_bytes=60 << 20
        ),
        cost_estimate=pl.CostEstimate(
            flops=15_000_000_000, bytes_accessed=40_000_000, transcendentals=13_000_000
        ),
        name="attention_sublayer",
    )(
        hidden_in, positions[None, :], frequencies, modulation, jnp.transpose(w_qkv, (1, 0, 2)), qk_gain, w_out,
        jnp.transpose(stale_kv, (1, 0, 2)),
    )


def solution(mesh):
    return jax.shard_map(
        local,
        mesh=mesh,
        in_specs=(
            P("patch", "head"),
            P("patch"),
            P(),
            P(None, None, "head"),
            P(None, "head"),
            P("head", None),
            P("patch", None, "head"),
        ),
        out_specs=P("patch", "head"),
        check_vma=False,
    )
```

time: 144 us -> 119 us (0.83)
  the two profiles are of different devices: /device:TPU:1 before, /device:TPU:0 now
where the time goes in v2:
time: 119 us
  Pallas kernels  115 us (97%)
  local copies, waits for them, and re-layouts  4.09 us (3%)
    pallas_call x1, Pallas kernels, local(): pl.pallas_call(kernel, out_shape=jax.ShapeDtypeStruct((ROWS, COLS), bf16)...  115 us
    unnamed x2, local copies, waits for them, and re-layouts  4.09 us

profile of v2, /device:TPU:0, one launch (start us, length us, event | category | flops | bytes accessed | tf_op | source)
XLA Modules:
  0.0 119.2 jit_solution(14829353471069323255)
XLA Ops:
  0.0 0.6 maximum_bitcast_fusion.freq
  0.6 2.1 %copy.10 = bf16[512,2,384]{2,0,1:T(8,128)(2,1)} copy(bf16[512,2,384]{2,1,0:T(2,128)(2,1)} %param.13) | data formatting | bytes 1572864 | tf_op args[6]
  2.7 114.5 %attention_sublayer.1 = bf16[512,640]{1,0:T(8,128)(2,1)} custom-call(bf16[512,640]{1,0:T(8,128)(2,1)} %hid_in.1, s32[1,512]{1,0:T(1,128)} %bitcast.9, f32[1,128]{1,0:T(1,128)} %maximum_bitcast_fusion.freq, f32[3,5120]{1,0:T(4,128)} %modulation.1, bf16[3,5120,384]{2,1,0:T(8,128)(2,1)} %bitcast.8, f32[2,384]{1,0:T(2,128)} %gain.1, bf16[384,5120]{1,0:T(8,128)(2,1)} %wout_in.1, ...), custom_call_target="tpu_custom_call" | custom-call | flops 15000000512 | bytes 40000000 | tf_op jit(solution)/shard_map/attention_sublayer/pallas_call | solution.py:389
  117.2 2.0 %copy.12 = bf16[512,640]{1,0:T(8,128)(2,1)} copy(bf16[512,640]{1,0:T(8,128)(2,1)} %attention_sublayer.1) | data formatting | bytes 1310720
  (1 shorter events, 0.0 us)

commit v3 on v2

--- a/solution.py
+++ b/solution.py
@@ -19,8 +19,9 @@
 EXP_SCALE = HD ** (-0.5) * math.log2(math.e)
 MESH = pl.DeviceIdType.MESH
 NT = (((1,), (1,)), ((), ()))
-PEERS = (6, 2, 5, 7, 1, 3, 4)
+PEERS = (6, 2, 5, 7, 4, 1, 3)
 WO_SLOT = (0, 1, 4, 2, 3, 5, 6, 7)
+NEAR, FAR = 5, slice(3, 8)
 ORDER = (
     (0, 0, 1), (1, 0, 0), (1, 0, 1), (3, 0, 0), (3, 0, 1), (2, 0, 0), (2, 0, 1), (0, 1, 0),
     (0, 1, 1), (1, 1, 0), (1, 1, 1), (3, 1, 0), (3, 1, 1), (2, 1, 0), (2, 1, 1), (0, 0, 0),
@@ -107,27 +108,32 @@
     low = lambda t: pl.ds(t * TILE, TILE // 2)
     high = lambda t: pl.ds(t * TILE + TILE // 2, TILE // 2)
 
-    def spread(buffer, source, t):
+    every = slice(None)
+
+    def spread(buffer, source, t, cols=every):
         return {
-            rel: ship(source.at[part(t)], buffer.at[mirrored(rel), part(t)], place(rel=rel))
-            for rel in (1, 3, 4)
+            rel: ship(
+                source.at[part(t), cols], buffer.at[mirrored(rel), part(t), cols], place(rel=rel)
+            )
+            for rel in (4, 1, 3)
         }
 
-    def relay(buffer, near, t):
+    def onward(buffer, near, t, cols=every):
         arrive(near[1], near[3])
-        far = (
-            ship(buffer.at[3, low(t)], buffer.at[2, low(t)], place(rel=1)),
-            ship(buffer.at[1, high(t)], buffer.at[2, high(t)], place(rel=3)),
-        )
+        return (
+            ship(buffer.at[3, low(t), cols], buffer.at[2, low(t), cols], place(rel=1)),
+            ship(buffer.at[1, high(t), cols], buffer.at[2, high(t), cols], place(rel=3)),
+        )
+
+    def sideways(buffer, near, t, cols=every):
         arrive(near[4])
-        side = (
-            ship(buffer.at[4, part(t)], buffer.at[7, part(t)], place(rel=1)),
-            ship(buffer.at[4, part(t)], buffer.at[5, part(t)], place(rel=3)),
-        )
-        return far, side
-
-    def across_y(buffer, far, side, t):
-        arrive(*far, *side)
+        return (
+            ship(buffer.at[4, part(t), cols], buffer.at[7, part(t), cols], place(rel=1)),
+            ship(buffer.at[4, part(t), cols], buffer.at[5, part(t), cols], place(rel=3)),
+        )
+
+    def across_y(buffer, side, t):
+        arrive(*side)
         return (
             ship(buffer.at[7, low(t)], buffer.at[6, low(t)], place(rel=1)),
             ship(buffer.at[5, high(t)], buffer.at[6, high(t)], place(rel=3)),
@@ -155,6 +161,11 @@
     lane = lax.broadcasted_iota(jnp.int32, (ROWS, HD), 1)
     cosine[...] = jnp.cos(angles)
     sine[...] = jnp.where(lane < HD // 2, -1.0, 1.0) * jnp.sin(angles)
+
+    far[0] = onward(hid, near[0], 0)
+    side[0] = sideways(hid, near[0], 0)
+    near[1] = spread(hid, hid_in, 1)
+    kv_x = ship(kv_in, kv.at[SLOT[0, 1, 0]], place(dxh=1))
 
     arrive(*stat_copies)
     sums = sum(stats[r, 0:1, :] for r in range(8))
@@ -214,10 +225,11 @@
                 else:
                     kv[OWN, 0, rows, cols] = turned.astype(jnp.bfloat16)
 
-    def attend(t, first, slots):
+    def attend(t, first, slots, heads=tuple(range(HEADS_DEV))):
         rows = slice(t * TILE, t * TILE + TILE)
         columns = [slice(h * HD, h * HD + HD) for h in range(HEADS_DEV)]
-        for h, cols in enumerate(columns):
+        for h in heads:
+            cols = columns[h]
             if first == 0:
                 run_max[h, rows] = jnp.full((TILE, 128), -1e30, jnp.float32)
                 run_sum[h, rows] = jnp.zeros((TILE, 128), jnp.float32)
@@ -228,7 +240,8 @@
             for u in range(2):
                 slot = first + 2 * i + u
                 after = jnp.minimum(slot + 1, first + slots - 1)
-                for h, cols in enumerate(columns):
+                for h in heads:
+                    cols = columns[h]
                     score[1 - u, h] = dot_nt(q[h, rows], kv[after, 0, :, cols])
                     now = score[u, h]
                     peak = now[:, :128]
@@ -251,17 +264,20 @@
 
         lax.fori_loop(0, slots // 2, body, 0)
 
-    def publish(t):
-        rows = slice(t * TILE, t * TILE + TILE)
-        for h in range(HEADS_DEV):
+    def publish(t, heads):
+        rows = slice(t * TILE, t * TILE + TILE)
+        for h in heads:
             att[0, rows, h * HD : h * HD + HD] = (
                 run_acc[h, rows] / jnp.sum(run_sum[h, rows], axis=1, keepdims=True)
             ).astype(jnp.bfloat16)
-        return spread(att, att.at[0], t)
-
-    def across_x(far, t):
+        return spread(att, att.at[0], t, span(heads))
+
+    def span(heads):
+        return slice(heads[0] * HD, heads[-1] * HD + HD)
+
+    def across_x(far, t, cols=every):
         arrive(*far)
-        return ship(att.at[2, part(t)], att.at[6, part(t)], place(rel=4))
+        return ship(att.at[2, part(t), cols], att.at[6, part(t), cols], place(rel=4))
 
     def output(r, t):
         rows = slice(t * TILE, t * TILE + TILE)
@@ -273,10 +289,10 @@
 
     for t in range(2):
         project(0, t)
-    far[0], side[0] = relay(hid, near[0], 0)
-    kv_x = ship(kv_in, kv.at[SLOT[0, 1, 0]], place(dxh=1))
     for rel in (1, 3, 4):
         project(rel, 0)
+    arrive(*far[0])
+    project(2, 0)
     arrive(kv_z[1], kv_z[3])
     up, down, two = SLOT[3, 0, 0], SLOT[1, 0, 0], SLOT[2, 0, 0]
     kv_far = (
@@ -284,16 +300,11 @@
         ship(kv.at[down, 1], kv.at[two, 1], place(dz=3)),
     )
     kv_core[3, 0], kv_core[1, 0] = pass_to_core((3, 0)), pass_to_core((1, 0))
-    opp[0] = across_y(hid, far[0], side[0], 0)
-    for rel in (2, 5, 7):
+    far[1] = onward(hid, near[1], 1)
+    opp[0] = across_y(hid, side[0], 0)
+    side[1] = sideways(hid, near[1], 1)
+    for rel in (5, 7):
         project(rel, 0)
-    near[1] = spread(hid, hid_in, 1)
-    arrive(*opp[0])
-    project(6, 0)
-    norm_copies = send_norms(0)
-    arrive(*kv_far)
-    kv_core[2, 0] = pass_to_core((2, 0))
-    kv_x_far = ship(kv.at[two], kv.at[SLOT[2, 1, 0]], place(dxh=1))
     arrive(kv_x)
     beside = SLOT[0, 1, 0]
     kv_x_z = (
@@ -301,76 +312,111 @@
         ship(kv.at[beside], kv.at[SLOT[1, 1, 0]], place(dz=3)),
     )
     kv_core[0, 1] = pass_to_core((0, 1))
-    finish_projection(0, norm_copies)
-    far[1], side[1] = relay(hid, near[1], 1)
     for rel in (1, 3, 4):
         project(rel, 1)
-    arrive(kv_core[0, 0], kv_core[1, 0], kv_core[3, 0], kv_core[2, 0])
-    attend(0, 0, 8)
-    opp[1] = across_y(hid, far[1], side[1], 1)
-    for rel in (2, 5, 7):
-        project(rel, 1)
+    arrive(*kv_far)
+    kv_core[2, 0] = pass_to_core((2, 0))
+    kv_x_far = [ship(kv.at[two, 0], kv.at[SLOT[2, 1, 0], 0], place(dxh=1))]
+    arrive(*opp[0])
+    project(6, 0)
+    norm_copies = send_norms(0)
+    arrive(*far[1])
+    project(2, 1)
+    opp[1] = across_y(hid, side[1], 1)
+    finish_projection(0, norm_copies)
     HALF, EIGHTH = WIDTH // 2, WIDTH // 8
     half = pl.ds(pl.multiple_of(core * HALF, HALF), HALF)
     share = lambda dz: pl.ds(
         pl.multiple_of((((z + dz) % 4) * 2 + core) * EIGHTH, EIGHTH), EIGHTH
     )
+
+    def send_weights(r, rows):
+        to = place(rel=r)
+        cols = pl.ds(pl.multiple_of(to[1] * COLS, COLS), COLS)
+        return ship(wout_in.at[rows, cols], wo.at[WO_SLOT[mirrored(r)], rows], to)
+
+    wo_copies = [send_weights(r, share(0)) for r in PEERS[:NEAR]]
+    arrive(kv_core[0, 0], kv_core[1, 0], kv_core[3, 0], kv_core[2, 0])
+    attend(0, 0, 8)
+    for rel in (5, 7):
+        project(rel, 1)
     arrive(*opp[1])
     project(6, 1)
     norm_copies = send_norms(1)
-    wo_copies = []
-    for r in PEERS:
-        to = place(rel=r)
-        rows = half if r in (1, 3, 4) else share(0)
-        cols = pl.ds(pl.multiple_of(to[1] * COLS, COLS), COLS)
-        wo_copies.append(ship(wout_in.at[rows, cols], wo.at[WO_SLOT[mirrored(r)], rows], to))
     arrive(*kv_x_z)
+    above, below, last = SLOT[3, 1, 0], SLOT[1, 1, 0], SLOT[2, 1, 0]
+    kv_x_far += [
+        ship(kv.at[above, 1, part(0)], kv.at[last, 1, part(0)], place(dz=1)),
+        ship(kv.at[below, 1, part(1)], kv.at[last, 1, part(1)], place(dz=3)),
+    ]
     kv_core[3, 1], kv_core[1, 1] = pass_to_core((3, 1)), pass_to_core((1, 1))
-    arrive(kv_x_far)
+    finish_projection(1, norm_copies)
+    wo_copies += [send_weights(r, half) for r in PEERS[NEAR:]]
+    attend(1, 0, 8)
+    arrive(*kv_x_far)
     kv_core[2, 1] = pass_to_core((2, 1))
-    finish_projection(1, norm_copies)
-    attend(1, 0, 8)
-    arrive(*wo_copies)
-    wo_z = [ship(wo.at[4:8, share(0)], wo.at[4:8, share(0)], place(dz=dz)) for dz in (1, 3)]
-    wo_core = [
-        ship(wo.at[1:4, half], wo.at[1:4, half], place(dcore=1)),
-        ship(wo.at[4:8, share(0)], wo.at[4:8, share(0)], place(dcore=1)),
-    ]
+    arrive(*wo_copies[:NEAR])
+    wo_z = [ship(wo.at[FAR, share(0)], wo.at[FAR, share(0)], place(dz=dz)) for dz in (1, 3)]
+    wo_core = [ship(wo.at[FAR, share(0)], wo.at[FAR, share(0)], place(dcore=1))]
     arrive(kv_core[0, 1], kv_core[1, 1], kv_core[3, 1], kv_core[2, 1])
-    attend(0, 8, 8)
-    att_near = {0: publish(0)}
-    att_far, att_side, att_opp = {}, {}, {}
-    attend(1, 8, 4)
-    att_far[0], att_side[0] = relay(att, att_near[0], 0)
+    parts = ((0, (0, 1)), (0, (2,)), (1, (0, 1)), (1, (2,)))
+    att_near, att_far, att_side, att_opp = {}, {}, {}, {}
+
+    def attend_and_publish(i):
+        t, heads = parts[i]
+        attend(t, 8, 8, heads)
+        att_near[i] = publish(t, heads)
+
+    def first_relay(i):
+        t, heads = parts[i]
+        att_far[i] = onward(att, att_near[i], t, span(heads))
+        att_side[i] = sideways(att, att_near[i], t, span(heads))
+
+    def second_relay(i):
+        t, heads = parts[i]
+        att_opp[i] = across_x(att_far[i], t, span(heads))
+
+    attend_and_publish(0)
+    attend_and_publish(1)
+    first_relay(0)
+    attend_and_publish(2)
+    first_relay(1)
+    second_relay(0)
+    arrive(*wo_copies[NEAR:])
+    wo_core.append(ship(wo.at[1:3, half], wo.at[1:3, half], place(dcore=1)))
     arrive(*wo_z)
     wo_far = (
-        ship(wo.at[4:6, share(3)], wo.at[4:6, share(3)], place(dz=1)),
-        ship(wo.at[6:8, share(1)], wo.at[6:8, share(1)], place(dz=3)),
+        ship(wo.at[3:5, share(3)], wo.at[3:5, share(3)], place(dz=1)),
+        ship(wo.at[5:8, share(1)], wo.at[5:8, share(1)], place(dz=3)),
     )
     for dz in (1, 3):
-        wo_core.append(ship(wo.at[4:8, share(dz)], wo.at[4:8, share(dz)], place(dcore=1)))
-    attend(1, 12, 4)
-    att_near[1] = publish(1)
-    att_opp[0] = across_x(att_far[0], 0)
-    arrive(*wo_far)
-    wo_core.append(ship(wo.at[4:8, share(2)], wo.at[4:8, share(2)], place(dcore=1)))
+        wo_core.append(ship(wo.at[FAR, share(dz)], wo.at[FAR, share(dz)], place(dcore=1)))
+    attend_and_publish(3)
+    first_relay(2)
+    second_relay(1)
     load_wo.wait()
     output(0, 0)
     output(0, 1)
-    att_far[1], att_side[1] = relay(att, att_near[1], 1)
-    arrive(*wo_core)
-    for r in (1, 3, 4, 2):
+    arrive(*wo_far)
+    wo_core.append(ship(wo.at[FAR, share(2)], wo.at[FAR, share(2)], place(dcore=1)))
+    first_relay(3)
+    second_relay(2)
+    arrive(wo_core[1])
+    for r in (1, 3):
         output(r, 0)
-    att_opp[1] = across_x(att_far[1], 1)
-    arrive(*att_side[0], att_opp[0])
+        output(r, 1)
+    second_relay(3)
+    arrive(wo_core[0], *wo_core[2:])
+    for r in (4, 2):
+        output(r, 0)
+        output(r, 1)
+    arrive(*att_side[0], *att_side[1], att_opp[0], att_opp[1])
     for r in (5, 7, 6):
         output(r, 0)
-    for r in (1, 3, 4, 2):
-        output(r, 1)
-    arrive(*att_side[1])
+    arrive(*att_side[2], *att_side[3])
     output(5, 1)
     output(7, 1)
-    arrive(att_opp[1])
+    arrive(att_opp[2], att_opp[3])
     output(6, 1)
     gate = modulation[2:3, own_cols]
     out[...] = (hid[0].astype(jnp.float32) + gate * total[...]).astype(jnp.bfloat16)
@@ -385,7 +431,7 @@
     vmem = pl.BlockSpec(memory_space=pltpu.VMEM)
     hbm = pl.BlockSpec(memory_space=pl.ANY)
     f32, bf16 = jnp.float32, jnp.bfloat16
-    copies = 100
+    copies = 120
     return pl.pallas_call(
         kernel,
         out_shape=jax.ShapeDtypeStruct((ROWS, COLS), bf16),

time: 119 us -> 111 us (0.933)
  the two profiles are of different devices: /device:TPU:0 before, /device:TPU:1 now
where the time goes in v3:
time: 111 us
  Pallas kernels  106 us (95%)
  local copies, waits for them, and re-layouts  4.09 us (4%)
    pallas_call x1, Pallas kernels, local(): pl.pallas_call(kernel, out_shape=jax.ShapeDtypeStruct((ROWS, COLS), bf16)...  106 us
    unnamed x2, local copies, waits for them, and re-layouts  4.09 us

profile of v3, /device:TPU:1, one launch (start us, length us, event | category | flops | bytes accessed | tf_op | source)
XLA Modules:
  0.0 111.2 jit_solution(13335391850846126947)
XLA Ops:
  0.0 0.6 maximum_bitcast_fusion.freq
  0.6 2.1 %copy.10 = bf16[512,2,384]{2,0,1:T(8,128)(2,1)} copy(bf16[512,2,384]{2,1,0:T(2,128)(2,1)} %param.13) | data formatting | bytes 1572864 | tf_op args[6]
  2.7 106.5 %attention_sublayer.1 = bf16[512,640]{1,0:T(8,128)(2,1)} custom-call(bf16[512,640]{1,0:T(8,128)(2,1)} %hid_in.1, s32[1,512]{1,0:T(1,128)} %bitcast.9, f32[1,128]{1,0:T(1,128)} %maximum_bitcast_fusion.freq, f32[3,5120]{1,0:T(4,128)} %modulation.1, bf16[3,5120,384]{2,1,0:T(8,128)(2,1)} %bitcast.8, f32[2,384]{1,0:T(2,128)} %gain.1, bf16[384,5120]{1,0:T(8,128)(2,1)} %wout_in.1, ...), custom_call_target="tpu_custom_call" | custom-call | flops 15000000512 | bytes 40000000 | tf_op jit(solution)/shard_map/attention_sublayer/pallas_call | solution.py:435
  109.2 2.0 %copy.12 = bf16[512,640]{1,0:T(8,128)(2,1)} copy(bf16[512,640]{1,0:T(8,128)(2,1)} %attention_sublayer.1) | data formatting | bytes 1310720
  (1 shorter events, 0.0 us)

commit v4 on v3

--- a/solution.py
+++ b/solution.py
@@ -234,35 +234,38 @@
                 run_max[h, rows] = jnp.full((TILE, 128), -1e30, jnp.float32)
                 run_sum[h, rows] = jnp.zeros((TILE, 128), jnp.float32)
                 run_acc[h, rows] = jnp.zeros((TILE, HD), jnp.float32)
-            score[0, h] = dot_nt(q[h, rows], kv[first, 0, :, cols])
+            for e in range(2):
+                score[0, h, e] = dot_nt(q[h, rows], kv[first + e, 0, :, cols])
 
         def body(i, carry):
             for u in range(2):
-                slot = first + 2 * i + u
-                after = jnp.minimum(slot + 1, first + slots - 1)
+                slot = first + 4 * i + 2 * u
+                after = jnp.minimum(slot + 2, first + slots - 2)
                 for h in heads:
                     cols = columns[h]
-                    score[1 - u, h] = dot_nt(q[h, rows], kv[after, 0, :, cols])
-                    now = score[u, h]
-                    peak = now[:, :128]
-                    for g in range(1, 4):
-                        peak = jnp.maximum(peak, now[:, g * 128 : g * 128 + 128])
+                    for e in range(2):
+                        score[1 - u, h, e] = dot_nt(q[h, rows], kv[after + e, 0, :, cols])
+                    now = [
+                        score[u, h, e, :, g * 128 : g * 128 + 128]
+                        for e in range(2)
+                        for g in range(4)
+                    ]
+                    peak = functools.reduce(jnp.maximum, now)
                     old = run_max[h, rows]
                     new = jnp.maximum(old, jnp.max(peak, axis=1, keepdims=True))
                     fade = jnp.exp2((old - new) * EXP_SCALE)
-                    tally = run_sum[h, rows] * fade
-                    pieces = []
-                    for g in range(4):
-                        weight = jnp.exp2((now[:, g * 128 : g * 128 + 128] - new) * EXP_SCALE)
-                        tally = tally + weight
-                        pieces.append(weight.astype(jnp.bfloat16))
-                    weights = jnp.concatenate(pieces, axis=1)
-                    run_acc[h, rows] = run_acc[h, rows] * fade + dot(weights, kv[slot, 1, :, cols])
+                    weights = [jnp.exp2((piece - new) * EXP_SCALE) for piece in now]
+                    run_sum[h, rows] = run_sum[h, rows] * fade + sum(weights)
+                    rounded = [piece.astype(jnp.bfloat16) for piece in weights]
+                    gained = sum(
+                        dot(jnp.concatenate(rounded[4 * e : 4 * e + 4], axis=1), kv[slot + e, 1, :, cols])
+                        for e in range(2)
+                    )
+                    run_acc[h, rows] = run_acc[h, rows] * fade + gained
                     run_max[h, rows] = new
-                    run_sum[h, rows] = tally
             return carry
 
-        lax.fori_loop(0, slots // 2, body, 0)
+        lax.fori_loop(0, slots // 4, body, 0)
 
     def publish(t, heads):
         rows = slice(t * TILE, t * TILE + TILE)
@@ -286,6 +289,11 @@
             total[rows] = term
         else:
             total[rows] += term
+
+    def finish(t):
+        rows = slice(t * TILE, t * TILE + TILE)
+        gate = modulation[2:3, own_cols]
+        out[rows] = (hid[0, rows].astype(jnp.float32) + gate * total[rows]).astype(jnp.bfloat16)
 
     for t in range(2):
         project(0, t)
@@ -413,13 +421,13 @@
     arrive(*att_side[0], *att_side[1], att_opp[0], att_opp[1])
     for r in (5, 7, 6):
         output(r, 0)
+    finish(0)
     arrive(*att_side[2], *att_side[3])
     output(5, 1)
     output(7, 1)
     arrive(att_opp[2], att_opp[3])
     output(6, 1)
-    gate = modulation[2:3, own_cols]
-    out[...] = (hid[0].astype(jnp.float32) + gate * total[...]).astype(jnp.bfloat16)
+    finish(1)
     for copy in copies:
         copy.wait_send()
 
@@ -456,7 +464,7 @@
             pltpu.VMEM((HEADS_DEV, ROWS, 128), f32),
             pltpu.VMEM((HEADS_DEV, ROWS, 128), f32),
             pltpu.VMEM((HEADS_DEV, ROWS, HD), f32),
-            pltpu.VMEM((2, HEADS_DEV, TILE, ROWS), f32),
+            pltpu.VMEM((2, HEADS_DEV, 2, TILE, ROWS), f32),
             pltpu.VMEM((ROWS, COLS), f32),
             pltpu.SemaphoreType.DMA((copies,)),
             pltpu.SemaphoreType.DMA((copies,)),

time: 111 us -> 111 us (level)
  no operation moved by 1% of the time
where the time goes in v4:
time: 111 us; the launch traced here: 110 us
  Pallas kernels  106 us (95%)
  local copies, waits for them, and re-layouts  4.09 us (4%)
    pallas_call x1, Pallas kernels, local(): pl.pallas_call(kernel, out_shape=jax.ShapeDtypeStruct((ROWS, COLS), bf16)...  106 us
    unnamed x2, local copies, waits for them, and re-layouts  4.09 us

profile of v4, /device:TPU:1, one launch (start us, length us, event | category | flops | bytes accessed | tf_op | source)
XLA Modules:
  0.0 110.4 jit_solution(12652226592288966818)
XLA Ops:
  0.0 0.6 maximum_bitcast_fusion.freq
  0.6 2.1 %copy.10 = bf16[512,2,384]{2,0,1:T(8,128)(2,1)} copy(bf16[512,2,384]{2,1,0:T(2,128)(2,1)} %param.13) | data formatting | bytes 1572864 | tf_op args[6]
  2.7 105.7 %attention_sublayer.1 = bf16[512,640]{1,0:T(8,128)(2,1)} custom-call(bf16[512,640]{1,0:T(8,128)(2,1)} %hid_in.1, s32[1,512]{1,0:T(1,128)} %bitcast.9, f32[1,128]{1,0:T(1,128)} %maximum_bitcast_fusion.freq, f32[3,5120]{1,0:T(4,128)} %modulation.1, bf16[3,5120,384]{2,1,0:T(8,128)(2,1)} %bitcast.8, f32[2,384]{1,0:T(2,128)} %gain.1, bf16[384,5120]{1,0:T(8,128)(2,1)} %wout_in.1, ...), custom_call_target="tpu_custom_call" | custom-call | flops 15000000512 | bytes 40000000 | tf_op jit(solution)/shard_map/attention_sublayer/pallas_call | solution.py:443
  108.4 2.0 %copy.12 = bf16[512,640]{1,0:T(8,128)(2,1)} copy(bf16[512,640]{1,0:T(8,128)(2,1)} %attention_sublayer.1) | data formatting | bytes 1310720
  (1 shorter events, 0.0 us)
